TPU v7x, 512 devices: a whole 4x4x16 slice. The times are simulated.
512 devices in a mesh: pipe: 4 (over z_hi), dp: 16 (over y, x), tensor: 8 (over z_lo, core).
Axes of the slice: x: 4, y: 4, z: 16 (z_hi: 4, z_lo: 4; z = z_hi * 4 + z_lo), core: 2. Of those that a mesh axis runs over, the one named last changes fastest.
Arguments:
- x_in: bfloat16 [4, 2, 16, 128, 1600], P('pipe', None, 'dp', 'tensor'), may hold values from -6 to 6
- out_grad: bfloat16 [2, 16, 128, 1600], P(None, 'dp'), may hold values from -6 to 6
- layer_scale: float32 [4, 1600], P('pipe'), may hold values from 0.05 to 1
- norm_gain: float32 [4, 1600], P('pipe'), may hold values from 0.5 to 1.5
- master: float32 [4, 1600, 8192], P('pipe', 'dp', 'tensor'), may hold values from -0.15625 to 0.15625
- moment_one: float32 [4, 1600, 8192], P('pipe', 'dp', 'tensor'), may hold values from -4 to 4
- moment_two: float32 [4, 1600, 8192], P('pipe', 'dp', 'tensor'), may hold values from 0.05 to 5
Outputs:
- input_grads: bfloat16 [4, 2, 16, 128, 1600], P('pipe', None, 'dp', 'tensor')
- new_master: float32 [4, 1600, 8192], P('pipe', 'dp', 'tensor')
- new_moment_one: float32 [4, 1600, 8192], P('pipe', 'dp', 'tensor')
- new_moment_two: float32 [4, 1600, 8192], P('pipe', 'dp', 'tensor')
- scale_grads: float32 [4, 2, 1600], P('pipe')
All inputs are finite; a program needn't handle non-finite values.
Results may differ from a plain program's by a relative error of at most 0.027.
Values may be sent and summed in bfloat16 or wider, within the bound.
A program may use at most 128 MiB of HBM per device.

v0:
```python
import math
import jax
import jax.numpy as jnp
from jax import lax
from jax.sharding import PartitionSpec as P

HD = 128
beta_one = 0.9
beta_two = 0.95
adam_eps = 1e-08
learn_rate = 0.001
weight_decay = 0.05
adam_step = 100.0
norm_eps = 1e-06


def from_behind(block, axis, distance):
    devices = range(lax.axis_size(axis))
    route = [(i - distance, i) for i in devices if i - distance in devices]
    return lax.ppermute(block, axis, route)


def normalize(values_in):
    inverse = lax.rsqrt(jnp.mean(values_in * values_in, axis=-1, keepdims=True) + norm_eps)
    return (inverse, values_in * inverse)


def select_micro(array, micro_index):
    return lax.dynamic_index_in_dim(array, micro_index, 0, keepdims=False)


def store_slot(buffer, value, slot_index):
    return lax.dynamic_update_index_in_dim(buffer, value, slot_index, 0)


def local(x_in, out_grad, layer_scale, norm_gain, master, moment_one, moment_two):
    n_pipe = lax.axis_size("pipe")
    n_tensor = lax.axis_size("tensor")
    pipe_rank = lax.axis_index("pipe")
    micro_count = x_in.shape[1]
    images = x_in.shape[2]
    shard_len = x_in.shape[3]
    channels = x_in.shape[4]
    seq_len = shard_len * n_tensor
    row_start = lax.axis_index("tensor") * shard_len
    head_cols = master.shape[2] // 4
    local_heads = head_cols // HD
    score_root = math.sqrt(HD)
    scale_vec = layer_scale[0]
    gain_vec = norm_gain[0]
    weights = lax.all_gather(master[0].astype(jnp.bfloat16), "dp", axis=0, tiled=True)
    w_qkv = weights[:, : 3 * head_cols]
    w_out = weights[:, 3 * head_cols :]
    full_x = lax.all_gather(x_in[0], "tensor", axis=2, tiled=True).astype(jnp.float32)
    full_inverse, full_unit = normalize(full_x)
    normed = (full_unit * gain_vec).astype(jnp.bfloat16)
    local_unit = lax.dynamic_slice_in_dim(full_unit, row_start, shard_len, 2)
    local_inverse = lax.dynamic_slice_in_dim(full_inverse, row_start, shard_len, 2)
    projected = jnp.einsum(
        "mbsd,dc->mbsc", normed, w_qkv, preferred_element_type=jnp.float32
    ).astype(jnp.bfloat16)
    projected = projected.reshape(micro_count, images, seq_len, 3, local_heads, HD)
    query = projected[:, :, :, 0]
    keys = projected[:, :, :, 1]
    values = projected[:, :, :, 2]
    scores = (
        jnp.einsum("mbqhe,mbkhe->mbhqk", query, keys, preferred_element_type=jnp.float32)
        / score_root
    )
    probs = jax.nn.softmax(scores, axis=-1)
    probs_low = probs.astype(jnp.bfloat16)
    attended = jnp.einsum(
        "mbhqk,mbkhe->mbqhe", probs_low, values, preferred_element_type=jnp.float32
    ).astype(jnp.bfloat16)
    attended_flat = attended.reshape(micro_count, images, seq_len, head_cols)

    def backward_segment(micro_index, incoming):
        query_now = select_micro(query, micro_index)
        keys_now = select_micro(keys, micro_index)
        values_now = select_micro(values, micro_index)
        probs_now = select_micro(probs, micro_index)
        probs_low_now = select_micro(probs_low, micro_index)
        attended_now = select_micro(attended, micro_index)
        scaled = (scale_vec * incoming.astype(jnp.float32)).astype(jnp.bfloat16)
        d_att = jnp.einsum("bsd,dc->bsc", scaled, w_out, preferred_element_type=jnp.float32).astype(
            jnp.bfloat16
        )
        d_att = d_att.reshape(images, seq_len, local_heads, HD)
        d_prob = jnp.einsum(
            "bqhe,bkhe->bhqk", d_att, values_now, preferred_element_type=jnp.float32
        )
        row_delta = jnp.einsum(
            "bqhe,bqhe->bhq", d_att, attended_now, preferred_element_type=jnp.float32
        )
        d_score = (probs_now * (d_prob - row_delta[..., None]) / score_root).astype(jnp.bfloat16)
        d_query = jnp.einsum(
            "bhqk,bkhe->bqhe", d_score, keys_now, preferred_element_type=jnp.float32
        ).astype(jnp.bfloat16)
        d_keys = jnp.einsum(
            "bhqk,bqhe->bkhe", d_score, query_now, preferred_element_type=jnp.float32
        ).astype(jnp.bfloat16)
        d_values = jnp.einsum(
            "bhqk,bqhe->bkhe", probs_low_now, d_att, preferred_element_type=jnp.float32
        ).astype(jnp.bfloat16)
        d_proj = jnp.concatenate([d_query, d_keys, d_values], axis=2).reshape(
            images, seq_len, 3 * head_cols
        )
        partial_sum = jnp.einsum("bsc,dc->bsd", d_proj, w_qkv, preferred_element_type=jnp.float32)
        return (partial_sum, d_proj, scaled)

    def spare_segment(micro_index, incoming):
        return (
            jnp.zeros((images, seq_len, channels), jnp.float32),
            jnp.zeros((images, seq_len, 3 * head_cols), jnp.bfloat16),
            jnp.zeros((images, seq_len, channels), jnp.bfloat16),
        )

    segments = n_pipe + micro_count - 1
    is_last = pipe_rank == n_pipe - 1
    received = jnp.zeros((images, seq_len, channels), jnp.bfloat16)
    slots = micro_count + 1
    grads_out = jnp.zeros((slots, images, shard_len, channels), jnp.bfloat16)
    proj_saved = jnp.zeros((slots, images, seq_len, 3 * head_cols), jnp.bfloat16)
    scaled_saved = jnp.zeros((slots, images, seq_len, channels), jnp.bfloat16)
    grad_saved = jnp.zeros((slots, images, seq_len, channels), jnp.bfloat16)
    gain_part = jnp.zeros((channels,), jnp.float32)
    for segment_step in range(segments):
        micro_index = segment_step - (n_pipe - 1) + pipe_rank
        active = jnp.logical_and(micro_index >= 0, micro_index < micro_count)
        micro_index = jnp.clip(micro_index, 0, micro_count - 1)
        slot_index = jnp.where(active, micro_index, micro_count)
        arrived = received
        incoming = jnp.where(is_last, select_micro(out_grad, micro_index), arrived)
        partial_sum, d_proj, scaled = lax.cond(
            active, backward_segment, spare_segment, micro_index, incoming
        )
        pieces = partial_sum.astype(jnp.bfloat16).reshape(images, n_tensor, shard_len, channels)
        landed = lax.all_to_all(pieces, "tensor", split_axis=1, concat_axis=1, tiled=True)
        own_d = jnp.sum(landed.astype(jnp.float32), axis=1)
        own_unit = select_micro(local_unit, micro_index)
        own_inverse = select_micro(local_inverse, micro_index)
        d_unit = own_d * gain_vec
        d_input = own_inverse * (
            d_unit - own_unit * jnp.mean(d_unit * own_unit, axis=-1, keepdims=True)
        )
        own_incoming = lax.dynamic_slice_in_dim(incoming, row_start, shard_len, 1)
        own_passed = (own_incoming.astype(jnp.float32) + d_input).astype(jnp.bfloat16)
        gain_part = gain_part + jnp.where(active, jnp.sum(own_d * own_unit, axis=(0, 1)), 0.0)
        grads_out = store_slot(grads_out, own_passed, slot_index)
        proj_saved = store_slot(proj_saved, d_proj, slot_index)
        scaled_saved = store_slot(scaled_saved, scaled, slot_index)
        grad_saved = store_slot(grad_saved, incoming, slot_index)
        if segment_step + 1 < segments:
            moved = from_behind(own_passed, "pipe", -1)
            received = lax.all_gather(moved, "tensor", axis=1, tiled=True)
    grads_kept = grads_out[:micro_count]
    proj_kept = proj_saved[:micro_count]
    scaled_kept = scaled_saved[:micro_count]
    grad_kept = grad_saved[:micro_count]
    grad_qkv = jnp.einsum("mbsd,mbsc->dc", normed, proj_kept, preferred_element_type=jnp.float32)
    grad_out = jnp.einsum(
        "mbsd,mbsc->dc", scaled_kept, attended_flat, preferred_element_type=jnp.float32
    )
    weight_grad = lax.psum_scatter(
        jnp.concatenate([grad_qkv, grad_out], axis=1).astype(jnp.bfloat16),
        "dp",
        scatter_dimension=0,
        tiled=True,
    ).astype(jnp.float32)
    summed_out = jnp.einsum(
        "mbsd,mbsc->dc", grad_kept, attended_flat, preferred_element_type=jnp.float32
    )
    scale_part = jnp.sum(w_out.astype(jnp.float32) * summed_out, axis=1)
    scale_both = lax.psum(lax.psum(jnp.stack([scale_part, gain_part]), "tensor"), "dp")
    bias_one = 1.0 - beta_one**adam_step
    bias_two = 1.0 - beta_two**adam_step
    first_new = beta_one * moment_one[0] + (1.0 - beta_one) * weight_grad
    second_new = beta_two * moment_two[0] + (1.0 - beta_two) * weight_grad * weight_grad
    update = first_new / bias_one / (jnp.sqrt(second_new / bias_two) + adam_eps)
    master_new = master[0] - learn_rate * (update + weight_decay * master[0])
    return (grads_kept[None], master_new[None], first_new[None], second_new[None], scale_both[None])


def solution(mesh):
    placed = (
        P("pipe", None, "dp", "tensor", None),
        P(None, "dp", None, None),
        P("pipe", None),
        P("pipe", None),
        P("pipe", "dp", "tensor"),
        P("pipe", "dp", "tensor"),
        P("pipe", "dp", "tensor"),
    )
    return jax.shard_map(
        local,
        mesh=mesh,
        in_specs=placed,
        out_specs=(
            P("pipe", None, "dp", "tensor", None),
            P("pipe", "dp", "tensor"),
            P("pipe", "dp", "tensor"),
            P("pipe", "dp", "tensor"),
            P("pipe", None, None),
        ),
        check_vma=False,
    )
```

profile of v0, /device:TPU:128, one launch (start us, length us, event | category | flops | bytes accessed | tf_op | source)
XLA Modules:
  0.0 831.2 jit_solution(14182584001447104835)
XLA Ops:
  9.8 17.2 %all-gather = bf16[1,2,1,128,1600]{4,3,2,1,0:T(8,128)(2,1)S(1)} all-gather(bf16[1,2,1,16,1600]{4,3,2,1,0:T(8,128)(2,1)} %param.17), channel_id=2, replica_groups=mesh['pipe'=4,'dp'=16,'tensor'=8] {'tensor'}, dimensions={3}, use_global_device_ids=true | all-gather | bytes 921600 | tf_op jit(solution)/shard_map/all_gather | solution.py:54
  28.4 50.3 %all-gather.4.cloned.1.call-done = bf16[16,100,1024]{2,1,0:T(8,128)(2,1)} async-done(((bf16[1,100,1024]{2,1,0:T(8,128)(2,1)}), bf16[16,100,1024]{2,1,0:T(8,128)(2,1)}) %all-gather.4.cloned.1.call-update) | async-done | bytes 3276816 | tf_op jit(solution)/shard_map/all_gather | solution.py:51
  78.8 4.5 reshape.1362
  84.5 2.6 fusion.115
  95.5 2.3 conditional.5
  99.8 4.8 all-to-all-start
  106.1 2.5 convert_multiply_fusion.6
  108.6 9.3 %all-to-all-done = bf16[1,8,16,1600]{3,2,0,1:T(8,128)(2,1)} async-done(((bf16[1,8,16,1600]{3,2,0,1:T(8,128)(2,1)}), bf16[1,8,16,1600]{3,2,0,1:T(8,128)(2,1)}, u32[]{:S(2)}, u32[]{:S(2)}) %all-to-all-start) | async-done | bytes 409632 | tf_op jit(solution)/shard_map/all_to_all | solution.py:138
  121.8 2.2 fusion.165
  132.2 40.1 %collective-permute-done = bf16[1,16,1600]{1,2,0:T(8,128)(2,1)} collective-permute-done((bf16[1,16,1600]{1,2,0:T(8,128)(2,1)}, bf16[1,16,1600]{1,2,0:T(8,128)(2,1)}, u32[]{:S(2)}, u32[]{:S(2)}) %collective-permute-start) | collective-permute-done | bytes 51232 | tf_op jit(solution)/shard_map/ppermute | solution.py:20
  174.1 15.8 %all_gather.20 = bf16[1,128,1600]{2,1,0:T(8,128)(2,1)} all-gather(bf16[1,16,1600]{2,1,0:T(8,128)(2,1)} %copy.219), channel_id=1, replica_groups=mesh['pipe'=4,'dp'=16,'tensor'=8] {'tensor'}, dimensions={1}, use_global_device_ids=true | all-gather | bytes 460800 | tf_op jit(solution)/shard_map/all_gather | solution.py:155
  194.0 2.7 conditional.6
  198.7 16.6 %all_to_all.25 = bf16[1,8,16,1600]{3,2,0,1:T(8,128)(2,1)S(1)} all-to-all(bf16[1,8,16,1600]{3,2,0,1:T(8,128)(2,1)} %bitcast.592), channel_id=1, replica_groups=mesh['pipe'=4,'dp'=16,'tensor'=8] {'tensor'}, dimensions={1} | all-to-all | bytes 819200 | tf_op jit(solution)/shard_map/all_to_all | solution.py:138
  228.6 94.0 %collective-permute-done.1 = bf16[1,16,1600]{1,2,0:T(8,128)(2,1)} collective-permute-done((bf16[1,16,1600]{1,2,0:T(8,128)(2,1)}, bf16[1,16,1600]{1,2,0:T(8,128)(2,1)}, u32[]{:S(2)}, u32[]{:S(2)}) %collective-permute-start.1) | collective-permute-done | bytes 51232 | tf_op jit(solution)/shard_map/ppermute | solution.py:20
  324.4 15.8 %all_gather.21 = bf16[1,128,1600]{2,1,0:T(8,128)(2,1)} all-gather(bf16[1,16,1600]{2,1,0:T(8,128)(2,1)} %copy.234), channel_id=1, replica_groups=mesh['pipe'=4,'dp'=16,'tensor'=8] {'tensor'}, dimensions={1}, use_global_device_ids=true | all-gather | bytes 460800 | tf_op jit(solution)/shard_map/all_gather | solution.py:155
  344.3 32.0 %conditional.7 = (bf16[1,128,1600]{1,2,0:T(8,128)(2,1)}, bf16[1,1,128,768]{3,2,0,1:T(8,128)(2,1)}, bf16[1,1,128,1600]{2,3,0,1:T(8,128)(2,1)}) conditional(s32[]{:T(128)} %convert_element_type.339, () %tuple.72, (s32[]{:T(128)}, bf16[2,1,128,2,128]{4,2,3,0,1:T(8,128)(2,1)}, f32[2,1,2,128,128]{3,4,2,0,1:T(8,128)S(1)}, f32[1,1600]{1,0:T(1,128)S(1)}, ...), branch_computations={%region_11.12_spmd, %region_12.13_spmd} | conditional | flops 454803200 | bytes 11565162 | solution.py:134
  378.3 4.1 all-to-all-start.2
  391.7 4.0 all-to-all-done.2
  411.1 38.8 %collective-permute-done.2 = bf16[1,16,1600]{1,2,0:T(8,128)(2,1)} collective-permute-done((bf16[1,16,1600]{1,2,0:T(8,128)(2,1)S(1)}, bf16[1,16,1600]{1,2,0:T(8,128)(2,1)}, u32[]{:S(2)}, u32[]{:S(2)}) %collective-permute-start.2) | collective-permute-done | bytes 51232 | tf_op jit(solution)/shard_map/ppermute | solution.py:20
  451.8 15.8 %all_gather.22 = bf16[1,128,1600]{2,1,0:T(8,128)(2,1)} all-gather(bf16[1,16,1600]{2,1,0:T(8,128)(2,1)} %copy.249), channel_id=1, replica_groups=mesh['pipe'=4,'dp'=16,'tensor'=8] {'tensor'}, dimensions={1}, use_global_device_ids=true | all-gather | bytes 460800 | tf_op jit(solution)/shard_map/all_gather | solution.py:155
  471.6 32.2 %conditional.8 = (bf16[1,128,1600]{1,2,0:T(8,128)(2,1)}, bf16[1,1,128,768]{3,2,0,1:T(8,128)(2,1)}, bf16[1,1,128,1600]{2,3,0,1:T(8,128)(2,1)}) conditional(s32[]{:T(128)} %convert_element_type.344, () %tuple.74, (s32[]{:T(128)}, bf16[2,1,128,2,128]{4,2,3,0,1:T(8,128)(2,1)}, f32[2,1,2,128,128]{3,4,2,0,1:T(8,128)S(1)}, f32[1,1600]{1,0:T(1,128)S(1)}, ...), branch_computations={%region_15.16_spmd, %region_16.17_spmd} | conditional | flops 454803200 | bytes 11565162 | solution.py:134
  505.9 4.1 all-to-all-start.3
  538.9 2.2 collective-permute-start.3
  544.3 14.5 %collective-permute-done.3 = bf16[1,16,1600]{1,2,0:T(8,128)(2,1)} collective-permute-done((bf16[1,16,1600]{1,2,0:T(8,128)(2,1)}, bf16[1,16,1600]{1,2,0:T(8,128)(2,1)}, u32[]{:S(2)}, u32[]{:S(2)}) %collective-permute-start.3) | collective-permute-done | bytes 51232 | tf_op jit(solution)/shard_map/ppermute | solution.py:20
  560.6 37.5 %all_gather.23 = bf16[1,128,1600]{2,1,0:T(8,128)(2,1)} all-gather(bf16[1,16,1600]{2,1,0:T(8,128)(2,1)} %copy.264), channel_id=1, replica_groups=mesh['pipe'=4,'dp'=16,'tensor'=8] {'tensor'}, dimensions={1}, use_global_device_ids=true | all-gather | bytes 460800 | tf_op jit(solution)/shard_map/all_gather | solution.py:155
  602.1 2.3 conditional.9
  606.5 5.1 all-to-all-start.4
  619.0 85.0 %fusion = bf16[112,1024]{1,0:T(8,128)(2,1)} fusion(bf16[1600,1024]{1,0:T(8,128)(2,1)S(1)} %pad_maximum_fusion.5), kind=kCustom, calls=%all-reduce-scatter | all-reduce-scatter fusion | flops 1835009 | bytes 3508224
  705.0 3.7 collective-permute-start.4
  708.6 4.1 collective-permute-start.5
  722.6 27.0 %psum.14 = f32[2,1600]{1,0:T(2,128)S(1)} all-reduce(f32[2,1600]{1,0:T(2,128)S(1)} %pad_maximum_fusion.6), channel_id=1, replica_groups=mesh['pipe'=4,'dp'=16,'tensor'=8] {'tensor'}, use_global_device_ids=true, to_apply=%region_30.31 | all-reduce | flops 3200 | bytes 25600 | tf_op jit(solution)/shard_map/psum | solution.py:174
  749.6 71.2 %psum.15 = f32[1,2,1600]{2,1,0:T(2,128)} all-reduce(f32[1,2,1600]{2,1,0:T(2,128)S(1)} %bitcast.594), channel_id=1, replica_groups=mesh['pipe'=4,'dp'=16,'tensor'=8] {'dp'}, use_global_device_ids=true, to_apply=%region_31.32 | all-reduce | flops 3200 | bytes 25600 | tf_op jit(solution)/shard_map/psum | solution.py:174
  (240 shorter events, 222.2 us)
Async XLA Ops:
  7.2 71.6 %all-gather.4.cloned.1.call-start = ((), (), s32[]{:S(2)}) async-start(), calls=%async_computation.5 | async-start | bytes 3620864 | tf_op jit(solution)/shard_map/all_gather | solution.py:51
  9.0 18.5 %copy-start.10 = (bf16[2,1,128,1600]{2,3,1,0:T(8,128)(2,1)S(1)}, bf16[2,1,128,1600]{2,3,1,0:T(8,128)(2,1)}, u32[]{:S(2)}) copy-start(bf16[2,1,128,1600]{2,3,1,0:T(8,128)(2,1)} %param.18) | copy-start | bytes 2457604
  27.0 57.4 %copy-start = (bf16[1,2,1,128,1600]{4,3,2,1,0:T(8,128)(2,1)}, bf16[1,2,1,128,1600]{4,3,2,1,0:T(8,128)(2,1)S(1)}, u32[]{:S(2)}) copy-start(bf16[1,2,1,128,1600]{4,3,2,1,0:T(8,128)(2,1)S(1)} %all-gather) | copy-start | bytes 2457604
  27.3 57.2 %copy-start.39 = (f32[2,128]{1,0:T(2,128)}, f32[2,128]{1,0:T(2,128)S(1)}, u32[]{:S(2)}) copy-start(f32[2,128]{1,0:T(2,128)S(1)} %add_rsqrt_fusion) | copy-start | bytes 3076
  28.4 50.4 %copy-start.21 = (bf16[3,1,128,1600]{2,3,0,1:T(8,128)(2,1)}, bf16[3,1,128,1600]{2,3,0,1:T(8,128)(2,1)S(1)}, u32[]{:S(2)}) copy-start(bf16[3,1,128,1600]{2,3,0,1:T(8,128)(2,1)S(1)} %get-tuple-element.409) | copy-start | bytes 3686404
  87.5 4.2 copy-start.26
  91.7 3.9 copy-start.33
  91.8 2.1 copy-start.12
  99.8 18.2 %all-to-all-start = ((bf16[1,8,16,1600]{3,2,0,1:T(8,128)(2,1)}), bf16[1,8,16,1600]{3,2,0,1:T(8,128)(2,1)}, u32[]{:S(2)}, u32[]{:S(2)}) async-start(bf16[1,8,16,1600]{3,2,0,1:T(8,128)(2,1)} %bitcast.589), calls=%async_computation | async-start | bytes 851968 | tf_op jit(solution)/shard_map/all_to_all | solution.py:138
  130.1 42.2 %collective-permute-start = (bf16[1,16,1600]{1,2,0:T(8,128)(2,1)}, bf16[1,16,1600]{1,2,0:T(8,128)(2,1)}, u32[]{:S(2)}, u32[]{:S(2)}) collective-permute-start(bf16[1,16,1600]{1,2,0:T(8,128)(2,1)} %fusion.121), channel_id=1, source_target_pairs={{128,0},{256,128},{384,256},{129,1},{257,129},{385,257},{130,2},{2... | collective-permute-start | bytes 153608 | tf_op jit(solution)/shard_map/ppermute | solution.py:20
  226.4 96.2 %collective-permute-start.1 = (bf16[1,16,1600]{1,2,0:T(8,128)(2,1)}, bf16[1,16,1600]{1,2,0:T(8,128)(2,1)}, u32[]{:S(2)}, u32[]{:S(2)}) collective-permute-start(bf16[1,16,1600]{1,2,0:T(8,128)(2,1)} %fusion.141), channel_id=1, source_target_pairs={{128,0},{256,128},{384,256},{129,1},{257,129},{385,257},{130,2},{2... | collective-permute-start | bytes 153608 | tf_op jit(solution)/shard_map/ppermute | solution.py:20
  378.3 17.4 %all-to-all-start.2 = ((bf16[1,8,16,1600]{3,2,0,1:T(8,128)(2,1)}), bf16[1,8,16,1600]{3,2,0,1:T(8,128)(2,1)}, u32[]{:S(2)}, u32[]{:S(2)}) async-start(bf16[1,8,16,1600]{3,2,0,1:T(8,128)(2,1)} %bitcast.590), calls=%async_computation.2 | async-start | bytes 851968 | tf_op jit(solution)/shard_map/all_to_all | solution.py:138
  405.7 4.8 copy-start.32
  407.9 42.0 %collective-permute-start.2 = (bf16[1,16,1600]{1,2,0:T(8,128)(2,1)S(1)}, bf16[1,16,1600]{1,2,0:T(8,128)(2,1)}, u32[]{:S(2)}, u32[]{:S(2)}) collective-permute-start(bf16[1,16,1600]{1,2,0:T(8,128)(2,1)S(1)} %fusion.136), channel_id=1, source_target_pairs={{128,0},{256,128},{384,256},{129,1},{257,129},{385,257},{130,2},{2... | collective-permute-start | bytes 153608 | tf_op jit(solution)/shard_map/ppermute | solution.py:20
  505.9 20.8 %all-to-all-start.3 = ((bf16[1,8,16,1600]{3,2,0,1:T(8,128)(2,1)}), bf16[1,8,16,1600]{3,2,0,1:T(8,128)(2,1)}, u32[]{:S(2)}, u32[]{:S(2)}) async-start(bf16[1,8,16,1600]{3,2,0,1:T(8,128)(2,1)} %bitcast.591), calls=%async_computation.3 | async-start | bytes 851968 | tf_op jit(solution)/shard_map/all_to_all | solution.py:138
  538.9 19.9 %collective-permute-start.3 = (bf16[1,16,1600]{1,2,0:T(8,128)(2,1)}, bf16[1,16,1600]{1,2,0:T(8,128)(2,1)}, u32[]{:S(2)}, u32[]{:S(2)}) collective-permute-start(bf16[1,16,1600]{1,2,0:T(8,128)(2,1)} %fusion.131), channel_id=1, source_target_pairs={{128,0},{256,128},{384,256},{129,1},{257,129},{385,257},{130,2},{2... | collective-permute-start | bytes 153608 | tf_op jit(solution)/shard_map/ppermute | solution.py:20
  604.4 8.8 %copy-start.1 = (bf16[1,2,1,128,1600]{4,3,2,1,0:T(8,128)(2,1)S(1)}, bf16[1,2,1,128,1600]{4,3,2,1,0:T(8,128)(2,1)}, u32[]{:S(2)}) copy-start(bf16[1,2,1,128,1600]{4,3,2,1,0:T(8,128)(2,1)} %copy-done) | copy-start | bytes 2457604
  604.4 8.8 %copy-start.40 = (f32[2,128]{1,0:T(2,128)S(1)}, f32[2,128]{1,0:T(2,128)}, u32[]{:S(2)}) copy-start(f32[2,128]{1,0:T(2,128)} %copy-done.39) | copy-start | bytes 3076
  606.5 113.7 %all-to-all-start.4 = ((bf16[1,8,16,1600]{3,2,0,1:T(8,128)(2,1)}), bf16[1,8,16,1600]{3,2,0,1:T(8,128)(2,1)}, u32[]{:S(2)}, u32[]{:S(2)}) async-start(bf16[1,8,16,1600]{3,2,0,1:T(8,128)(2,1)} %bitcast.152), calls=%async_computation.4 | async-start | bytes 851968 | tf_op jit(solution)/shard_map/all_to_all | solution.py:138
  613.2 3.7 copy-start.11
  704.0 11.5 %copy-start.20 = (bf16[112,1024]{1,0:T(8,128)(2,1)S(1)}, bf16[112,1024]{1,0:T(8,128)(2,1)}, u32[]{:S(2)}) copy-start(bf16[112,1024]{1,0:T(8,128)(2,1)} %fusion) | copy-start | bytes 688132
  705.0 10.5 %collective-permute-start.4 = (bf16[112,1024]{1,0:T(8,128)(2,1)}, bf16[112,1024]{1,0:T(8,128)(2,1)S(1)}, u32[]{:S(2)}, u32[]{:S(2)}) collective-permute-start(bf16[112,1024]{1,0:T(8,128)(2,1)} %fusion), channel_id=1, source_target_pairs={{0,8},{8,16},{16,24},{24,32},{32,40},{40,48},{48,56},{56,64},{64,7... | collective-permute-start | bytes 688136
  708.6 6.8 collective-permute-start.5
  712.7 3.4 copy-start.19
  712.7 3.4 copy-start.28
  712.7 3.4 copy-start.29
  717.8 4.7 copy-start.35
  717.8 4.7 copy-start.36
  717.8 4.7 copy-start.37
  717.8 4.7 copy-start.38
  722.2 99.2 %copy-start.13 = (bf16[1,128,1600]{1,2,0:T(8,128)(2,1)S(1)}, bf16[1,128,1600]{1,2,0:T(8,128)(2,1)}, u32[]{:S(2)}) copy-start(bf16[1,128,1600]{1,2,0:T(8,128)(2,1)} %get-tuple-element.402) | copy-start | bytes 1228804
  722.2 99.2 %copy-start.41 = (f32[16]{0:T(128)S(1)}, f32[16]{0:T(128)}, u32[]{:S(2)}) copy-start(f32[16]{0:T(128)} %get-tuple-element.429) | copy-start | bytes 196
  (15 other events, 19.7 us)
Sparse Core Ops, SparseCore 0:
  11.6 67.1 all-gather.3
where the time goes:
time: 842 us; the launch traced here: 831 us
  blocking collectives  302 us (36%)
  waiting for transfers between devices  252 us (30%)
  local copies, waits for them, and re-layouts  145 us (17%)
  other arithmetic  54.5 us (6%)
  starting transfers between devices  34.3 us (4%)
  matrix products  27.2 us (3%)
  between operations  15.5 us (2%)
    ppermute x4, waiting for transfers between devices, from_behind(): return lax.ppermute(block, axis, route)  187 us
    unnamed x1, blocking collectives  85 us
    all_gather x4, blocking collectives, local(): received = lax.all_gather(moved, 'tensor', axis=1, tiled=True)  84.8 us
    psum x1, blocking collectives, local(): lax.psum(lax.psum(jnp.stack([scale_part, gain_part]), 'tensor'), 'dp')  71.2 us
    all_gather x1, waiting for transfers between devices, local(): lax.all_gather(master[0].astype(jnp.bfloat16), 'dp', axis=0, tiled=True)  50.3 us
    another operation x23, local copies, waits for them, and re-layouts  32.2 us
    psum x1, blocking collectives, local(): lax.psum(jnp.stack([scale_part, gain_part]), 'tensor')  27 us
    dynamic_update_slice x15, local copies, waits for them, and re-layouts, store_slot(): return lax.dynamic_update_index_in_dim(buffer, value, slot_index, 0)  22.6 us
  transfers between devices with their start and end apart: 11, of which 8 were waited for; matrix products, arithmetic and copies ran while one was open for 16% of the time, Pallas kernels for 0%

commit v1 on v0

--- a/solution.py
+++ b/solution.py
@@ -171,7 +171,9 @@
         "mbsd,mbsc->dc", grad_kept, attended_flat, preferred_element_type=jnp.float32
     )
     scale_part = jnp.sum(w_out.astype(jnp.float32) * summed_out, axis=1)
-    scale_both = lax.psum(lax.psum(jnp.stack([scale_part, gain_part]), "tensor"), "dp")
+    scale_both = jnp.sum(
+        lax.all_gather(lax.psum(jnp.stack([scale_part, gain_part]), "tensor"), "dp"), axis=0
+    )
     bias_one = 1.0 - beta_one**adam_step
     bias_two = 1.0 - beta_two**adam_step
     first_new = beta_one * moment_one[0] + (1.0 - beta_one) * weight_grad

time: 842 us -> 796 us (0.945)
  blocking collectives: 302 us -> 255 us
    psum x1 -> x0, blocking collectives: 71.2 us -> none  [local(): lax.psum(lax.psum(jnp.stack([scale_part, gain_part]), 'tensor'), 'dp')]
    all_gather x0 -> x1, blocking collectives: none -> 24.6 us  [local(): lax.all_gather(lax.psum(jnp.stack([scale_part, gain_part]), 'tensor'), 'dp')]
  transfers between devices with their start and end apart: 11 -> 11, of which waited for: 8 -> 8; matrix products, arithmetic and copies ran while one was open for 16% -> 17% of each run, Pallas kernels for 0% -> 0%
where the time goes in v1:
time: 796 us; the launch traced here: 785 us
  blocking collectives  255 us (32%)
  waiting for transfers between devices  252 us (32%)
  local copies, waits for them, and re-layouts  145 us (18%)
  other arithmetic  55.2 us (7%)
  starting transfers between devices  34.3 us (4%)
  matrix products  27.2 us (3%)
  between operations  15.5 us (2%)
    ppermute x4, waiting for transfers between devices, from_behind(): return lax.ppermute(block, axis, route)  187 us
    unnamed x1, blocking collectives  85 us
    all_gather x4, blocking collectives, local(): received = lax.all_gather(moved, 'tensor', axis=1, tiled=True)  84.8 us
    all_gather x1, waiting for transfers between devices, local(): lax.all_gather(master[0].astype(jnp.bfloat16), 'dp', axis=0, tiled=True)  50.3 us
    another operation x23, local copies, waits for them, and re-layouts  32.2 us
    psum x1, blocking collectives, local(): lax.psum(jnp.stack([scale_part, gain_part]), 'tensor')  27 us
    all_gather x1, blocking collectives, local(): lax.all_gather(lax.psum(jnp.stack([scale_part, gain_part]), 'tensor'), 'dp')  24.6 us
    dynamic_update_slice x15, local copies, waits for them, and re-layouts, store_slot(): return lax.dynamic_update_index_in_dim(buffer, value, slot_index, 0)  22.6 us
  transfers between devices with their start and end apart: 11, of which 8 were waited for; matrix products, arithmetic and copies ran while one was open for 17% of the time, Pallas kernels for 0%

profile of v1, /device:TPU:128, one launch (start us, length us, event | category | flops | bytes accessed | tf_op | source)
XLA Modules:
  0.0 785.3 jit_solution(4144338740636004742)
XLA Ops:
  9.8 17.2 %all-gather = bf16[1,2,1,128,1600]{4,3,2,1,0:T(8,128)(2,1)S(1)} all-gather(bf16[1,2,1,16,1600]{4,3,2,1,0:T(8,128)(2,1)} %param.17), channel_id=2, replica_groups=mesh['pipe'=4,'dp'=16,'tensor'=8] {'tensor'}, dimensions={3}, use_global_device_ids=true | all-gather | bytes 921600 | tf_op jit(solution)/shard_map/all_gather | solution.py:54
  28.4 50.3 %all-gather.4.cloned.1.call-done = bf16[16,100,1024]{2,1,0:T(8,128)(2,1)} async-done(((bf16[1,100,1024]{2,1,0:T(8,128)(2,1)}), bf16[16,100,1024]{2,1,0:T(8,128)(2,1)}) %all-gather.4.cloned.1.call-update) | async-done | bytes 3276816 | tf_op jit(solution)/shard_map/all_gather | solution.py:51
  78.8 4.5 reshape.1362
  84.5 2.6 fusion.115
  95.5 2.3 conditional.5
  99.8 4.8 all-to-all-start
  106.1 2.5 convert_multiply_fusion.6
  108.6 9.3 %all-to-all-done = bf16[1,8,16,1600]{3,2,0,1:T(8,128)(2,1)} async-done(((bf16[1,8,16,1600]{3,2,0,1:T(8,128)(2,1)}), bf16[1,8,16,1600]{3,2,0,1:T(8,128)(2,1)}, u32[]{:S(2)}, u32[]{:S(2)}) %all-to-all-start) | async-done | bytes 409632 | tf_op jit(solution)/shard_map/all_to_all | solution.py:138
  121.8 2.2 fusion.165
  132.2 40.1 %collective-permute-done = bf16[1,16,1600]{1,2,0:T(8,128)(2,1)} collective-permute-done((bf16[1,16,1600]{1,2,0:T(8,128)(2,1)}, bf16[1,16,1600]{1,2,0:T(8,128)(2,1)}, u32[]{:S(2)}, u32[]{:S(2)}) %collective-permute-start) | collective-permute-done | bytes 51232 | tf_op jit(solution)/shard_map/ppermute | solution.py:20
  174.1 15.8 %all_gather.26 = bf16[1,128,1600]{2,1,0:T(8,128)(2,1)} all-gather(bf16[1,16,1600]{2,1,0:T(8,128)(2,1)} %copy.219), channel_id=1, replica_groups=mesh['pipe'=4,'dp'=16,'tensor'=8] {'tensor'}, dimensions={1}, use_global_device_ids=true | all-gather | bytes 460800 | tf_op jit(solution)/shard_map/all_gather | solution.py:155
  194.0 2.7 conditional.6
  198.7 16.6 %all_to_all.25 = bf16[1,8,16,1600]{3,2,0,1:T(8,128)(2,1)S(1)} all-to-all(bf16[1,8,16,1600]{3,2,0,1:T(8,128)(2,1)} %bitcast.594), channel_id=1, replica_groups=mesh['pipe'=4,'dp'=16,'tensor'=8] {'tensor'}, dimensions={1} | all-to-all | bytes 819200 | tf_op jit(solution)/shard_map/all_to_all | solution.py:138
  228.6 94.0 %collective-permute-done.1 = bf16[1,16,1600]{1,2,0:T(8,128)(2,1)} collective-permute-done((bf16[1,16,1600]{1,2,0:T(8,128)(2,1)}, bf16[1,16,1600]{1,2,0:T(8,128)(2,1)}, u32[]{:S(2)}, u32[]{:S(2)}) %collective-permute-start.1) | collective-permute-done | bytes 51232 | tf_op jit(solution)/shard_map/ppermute | solution.py:20
  324.4 15.8 %all_gather.27 = bf16[1,128,1600]{2,1,0:T(8,128)(2,1)} all-gather(bf16[1,16,1600]{2,1,0:T(8,128)(2,1)} %copy.234), channel_id=1, replica_groups=mesh['pipe'=4,'dp'=16,'tensor'=8] {'tensor'}, dimensions={1}, use_global_device_ids=true | all-gather | bytes 460800 | tf_op jit(solution)/shard_map/all_gather | solution.py:155
  344.3 32.0 %conditional.7 = (bf16[1,128,1600]{1,2,0:T(8,128)(2,1)}, bf16[1,1,128,768]{3,2,0,1:T(8,128)(2,1)}, bf16[1,1,128,1600]{2,3,0,1:T(8,128)(2,1)}) conditional(s32[]{:T(128)} %convert_element_type.339, () %tuple.72, (s32[]{:T(128)}, bf16[2,1,128,2,128]{4,2,3,0,1:T(8,128)(2,1)}, f32[2,1,2,128,128]{3,4,2,0,1:T(8,128)S(1)}, f32[1,1600]{1,0:T(1,128)S(1)}, ...), branch_computations={%region_11.12_spmd, %region_12.13_spmd} | conditional | flops 454803200 | bytes 11565162 | solution.py:134
  378.3 4.1 all-to-all-start.2
  391.7 4.0 all-to-all-done.2
  411.1 38.8 %collective-permute-done.2 = bf16[1,16,1600]{1,2,0:T(8,128)(2,1)} collective-permute-done((bf16[1,16,1600]{1,2,0:T(8,128)(2,1)S(1)}, bf16[1,16,1600]{1,2,0:T(8,128)(2,1)}, u32[]{:S(2)}, u32[]{:S(2)}) %collective-permute-start.2) | collective-permute-done | bytes 51232 | tf_op jit(solution)/shard_map/ppermute | solution.py:20
  451.8 15.8 %all_gather.28 = bf16[1,128,1600]{2,1,0:T(8,128)(2,1)} all-gather(bf16[1,16,1600]{2,1,0:T(8,128)(2,1)} %copy.249), channel_id=1, replica_groups=mesh['pipe'=4,'dp'=16,'tensor'=8] {'tensor'}, dimensions={1}, use_global_device_ids=true | all-gather | bytes 460800 | tf_op jit(solution)/shard_map/all_gather | solution.py:155
  471.6 32.2 %conditional.8 = (bf16[1,128,1600]{1,2,0:T(8,128)(2,1)}, bf16[1,1,128,768]{3,2,0,1:T(8,128)(2,1)}, bf16[1,1,128,1600]{2,3,0,1:T(8,128)(2,1)}) conditional(s32[]{:T(128)} %convert_element_type.344, () %tuple.74, (s32[]{:T(128)}, bf16[2,1,128,2,128]{4,2,3,0,1:T(8,128)(2,1)}, f32[2,1,2,128,128]{3,4,2,0,1:T(8,128)S(1)}, f32[1,1600]{1,0:T(1,128)S(1)}, ...), branch_computations={%region_15.16_spmd, %region_16.17_spmd} | conditional | flops 454803200 | bytes 11565162 | solution.py:134
  505.9 4.1 all-to-all-start.3
  538.9 2.2 collective-permute-start.3
  544.3 14.5 %collective-permute-done.3 = bf16[1,16,1600]{1,2,0:T(8,128)(2,1)} collective-permute-done((bf16[1,16,1600]{1,2,0:T(8,128)(2,1)}, bf16[1,16,1600]{1,2,0:T(8,128)(2,1)}, u32[]{:S(2)}, u32[]{:S(2)}) %collective-permute-start.3) | collective-permute-done | bytes 51232 | tf_op jit(solution)/shard_map/ppermute | solution.py:20
  560.6 37.5 %all_gather.29 = bf16[1,128,1600]{2,1,0:T(8,128)(2,1)} all-gather(bf16[1,16,1600]{2,1,0:T(8,128)(2,1)} %copy.264), channel_id=1, replica_groups=mesh['pipe'=4,'dp'=16,'tensor'=8] {'tensor'}, dimensions={1}, use_global_device_ids=true | all-gather | bytes 460800 | tf_op jit(solution)/shard_map/all_gather | solution.py:155
  602.1 2.3 conditional.9
  606.5 5.1 all-to-all-start.4
  619.0 85.0 %fusion = bf16[112,1024]{1,0:T(8,128)(2,1)} fusion(bf16[1600,1024]{1,0:T(8,128)(2,1)S(1)} %pad_maximum_fusion.5), kind=kCustom, calls=%all-reduce-scatter | all-reduce-scatter fusion | flops 1835009 | bytes 3508224
  705.0 3.7 collective-permute-start.4
  708.6 4.1 collective-permute-start.5
  722.6 27.0 %psum.7 = f32[1,2,1600]{2,1,0:T(2,128)S(1)} all-reduce(f32[1,2,1600]{2,1,0:T(2,128)S(1)} %maximum_bitcast_fusion), channel_id=1, replica_groups=mesh['pipe'=4,'dp'=16,'tensor'=8] {'tensor'}, use_global_device_ids=true, to_apply=%region_30.31 | all-reduce | flops 3200 | bytes 25600 | tf_op jit(solution)/shard_map/psum | solution.py:175
  749.6 24.6 %all_gather.31 = f32[16,2,1600]{2,1,0:T(2,128)S(1)} all-gather(f32[1,2,1600]{2,1,0:T(2,128)S(1)} %psum.7), channel_id=1, replica_groups=mesh['pipe'=4,'dp'=16,'tensor'=8] {'dp'}, dimensions={0}, use_global_device_ids=true | all-gather | bytes 217600 | tf_op jit(solution)/shard_map/all_gather | solution.py:175
  (241 shorter events, 222.8 us)
Async XLA Ops:
  7.2 71.6 %all-gather.4.cloned.1.call-start = ((), (), s32[]{:S(2)}) async-start(), calls=%async_computation.5 | async-start | bytes 3620864 | tf_op jit(solution)/shard_map/all_gather | solution.py:51
  9.0 18.5 %copy-start.10 = (bf16[2,1,128,1600]{2,3,1,0:T(8,128)(2,1)S(1)}, bf16[2,1,128,1600]{2,3,1,0:T(8,128)(2,1)}, u32[]{:S(2)}) copy-start(bf16[2,1,128,1600]{2,3,1,0:T(8,128)(2,1)} %param.18) | copy-start | bytes 2457604
  27.0 57.4 %copy-start = (bf16[1,2,1,128,1600]{4,3,2,1,0:T(8,128)(2,1)}, bf16[1,2,1,128,1600]{4,3,2,1,0:T(8,128)(2,1)S(1)}, u32[]{:S(2)}) copy-start(bf16[1,2,1,128,1600]{4,3,2,1,0:T(8,128)(2,1)S(1)} %all-gather) | copy-start | bytes 2457604
  27.3 57.2 %copy-start.39 = (f32[2,128]{1,0:T(2,128)}, f32[2,128]{1,0:T(2,128)S(1)}, u32[]{:S(2)}) copy-start(f32[2,128]{1,0:T(2,128)S(1)} %add_rsqrt_fusion) | copy-start | bytes 3076
  28.4 50.4 %copy-start.21 = (bf16[3,1,128,1600]{2,3,0,1:T(8,128)(2,1)}, bf16[3,1,128,1600]{2,3,0,1:T(8,128)(2,1)S(1)}, u32[]{:S(2)}) copy-start(bf16[3,1,128,1600]{2,3,0,1:T(8,128)(2,1)S(1)} %get-tuple-element.409) | copy-start | bytes 3686404
  87.5 4.2 copy-start.26
  91.7 3.9 copy-start.33
  91.8 2.1 copy-start.12
  99.8 18.2 %all-to-all-start = ((bf16[1,8,16,1600]{3,2,0,1:T(8,128)(2,1)}), bf16[1,8,16,1600]{3,2,0,1:T(8,128)(2,1)}, u32[]{:S(2)}, u32[]{:S(2)}) async-start(bf16[1,8,16,1600]{3,2,0,1:T(8,128)(2,1)} %bitcast.591), calls=%async_computation | async-start | bytes 851968 | tf_op jit(solution)/shard_map/all_to_all | solution.py:138
  130.1 42.2 %collective-permute-start = (bf16[1,16,1600]{1,2,0:T(8,128)(2,1)}, bf16[1,16,1600]{1,2,0:T(8,128)(2,1)}, u32[]{:S(2)}, u32[]{:S(2)}) collective-permute-start(bf16[1,16,1600]{1,2,0:T(8,128)(2,1)} %fusion.121), channel_id=1, source_target_pairs={{128,0},{256,128},{384,256},{129,1},{257,129},{385,257},{130,2},{2... | collective-permute-start | bytes 153608 | tf_op jit(solution)/shard_map/ppermute | solution.py:20
  226.4 96.2 %collective-permute-start.1 = (bf16[1,16,1600]{1,2,0:T(8,128)(2,1)}, bf16[1,16,1600]{1,2,0:T(8,128)(2,1)}, u32[]{:S(2)}, u32[]{:S(2)}) collective-permute-start(bf16[1,16,1600]{1,2,0:T(8,128)(2,1)} %fusion.141), channel_id=1, source_target_pairs={{128,0},{256,128},{384,256},{129,1},{257,129},{385,257},{130,2},{2... | collective-permute-start | bytes 153608 | tf_op jit(solution)/shard_map/ppermute | solution.py:20
  378.3 17.4 %all-to-all-start.2 = ((bf16[1,8,16,1600]{3,2,0,1:T(8,128)(2,1)}), bf16[1,8,16,1600]{3,2,0,1:T(8,128)(2,1)}, u32[]{:S(2)}, u32[]{:S(2)}) async-start(bf16[1,8,16,1600]{3,2,0,1:T(8,128)(2,1)} %bitcast.592), calls=%async_computation.2 | async-start | bytes 851968 | tf_op jit(solution)/shard_map/all_to_all | solution.py:138
  405.7 4.8 copy-start.32
  407.9 42.0 %collective-permute-start.2 = (bf16[1,16,1600]{1,2,0:T(8,128)(2,1)S(1)}, bf16[1,16,1600]{1,2,0:T(8,128)(2,1)}, u32[]{:S(2)}, u32[]{:S(2)}) collective-permute-start(bf16[1,16,1600]{1,2,0:T(8,128)(2,1)S(1)} %fusion.136), channel_id=1, source_target_pairs={{128,0},{256,128},{384,256},{129,1},{257,129},{385,257},{130,2},{2... | collective-permute-start | bytes 153608 | tf_op jit(solution)/shard_map/ppermute | solution.py:20
  505.9 20.8 %all-to-all-start.3 = ((bf16[1,8,16,1600]{3,2,0,1:T(8,128)(2,1)}), bf16[1,8,16,1600]{3,2,0,1:T(8,128)(2,1)}, u32[]{:S(2)}, u32[]{:S(2)}) async-start(bf16[1,8,16,1600]{3,2,0,1:T(8,128)(2,1)} %bitcast.593), calls=%async_computation.3 | async-start | bytes 851968 | tf_op jit(solution)/shard_map/all_to_all | solution.py:138
  538.9 19.9 %collective-permute-start.3 = (bf16[1,16,1600]{1,2,0:T(8,128)(2,1)}, bf16[1,16,1600]{1,2,0:T(8,128)(2,1)}, u32[]{:S(2)}, u32[]{:S(2)}) collective-permute-start(bf16[1,16,1600]{1,2,0:T(8,128)(2,1)} %fusion.131), channel_id=1, source_target_pairs={{128,0},{256,128},{384,256},{129,1},{257,129},{385,257},{130,2},{2... | collective-permute-start | bytes 153608 | tf_op jit(solution)/shard_map/ppermute | solution.py:20
  604.4 8.8 %copy-start.1 = (bf16[1,2,1,128,1600]{4,3,2,1,0:T(8,128)(2,1)S(1)}, bf16[1,2,1,128,1600]{4,3,2,1,0:T(8,128)(2,1)}, u32[]{:S(2)}) copy-start(bf16[1,2,1,128,1600]{4,3,2,1,0:T(8,128)(2,1)} %copy-done) | copy-start | bytes 2457604
  604.4 8.8 %copy-start.40 = (f32[2,128]{1,0:T(2,128)S(1)}, f32[2,128]{1,0:T(2,128)}, u32[]{:S(2)}) copy-start(f32[2,128]{1,0:T(2,128)} %copy-done.39) | copy-start | bytes 3076
  606.5 113.7 %all-to-all-start.4 = ((bf16[1,8,16,1600]{3,2,0,1:T(8,128)(2,1)}), bf16[1,8,16,1600]{3,2,0,1:T(8,128)(2,1)}, u32[]{:S(2)}, u32[]{:S(2)}) async-start(bf16[1,8,16,1600]{3,2,0,1:T(8,128)(2,1)} %bitcast.152), calls=%async_computation.4 | async-start | bytes 851968 | tf_op jit(solution)/shard_map/all_to_all | solution.py:138
  613.2 3.7 copy-start.11
  704.0 11.5 %copy-start.20 = (bf16[112,1024]{1,0:T(8,128)(2,1)S(1)}, bf16[112,1024]{1,0:T(8,128)(2,1)}, u32[]{:S(2)}) copy-start(bf16[112,1024]{1,0:T(8,128)(2,1)} %fusion) | copy-start | bytes 688132
  705.0 10.5 %collective-permute-start.4 = (bf16[112,1024]{1,0:T(8,128)(2,1)}, bf16[112,1024]{1,0:T(8,128)(2,1)S(1)}, u32[]{:S(2)}, u32[]{:S(2)}) collective-permute-start(bf16[112,1024]{1,0:T(8,128)(2,1)} %fusion), channel_id=1, source_target_pairs={{0,8},{8,16},{16,24},{24,32},{32,40},{40,48},{48,56},{56,64},{64,7... | collective-permute-start | bytes 688136
  708.6 6.8 collective-permute-start.5
  712.7 3.4 copy-start.19
  712.7 3.4 copy-start.28
  712.7 3.4 copy-start.29
  717.8 4.7 copy-start.35
  717.8 4.7 copy-start.36
  717.8 4.7 copy-start.37
  717.8 4.7 copy-start.38
  722.2 52.6 %copy-start.13 = (bf16[1,128,1600]{1,2,0:T(8,128)(2,1)S(1)}, bf16[1,128,1600]{1,2,0:T(8,128)(2,1)}, u32[]{:S(2)}) copy-start(bf16[1,128,1600]{1,2,0:T(8,128)(2,1)} %get-tuple-element.402) | copy-start | bytes 1228804
  722.2 52.6 %copy-start.41 = (f32[16]{0:T(128)S(1)}, f32[16]{0:T(128)}, u32[]{:S(2)}) copy-start(f32[16]{0:T(128)} %get-tuple-element.429) | copy-start | bytes 196
  (15 other events, 19.7 us)
Sparse Core Ops, SparseCore 0:
  11.6 67.1 all-gather.3
